TPU v7x, 512 devices: a whole 4x4x16 slice. The times are simulated.
512 devices in a mesh: row: 32 (over x, z_hi, core), col: 16 (over y, z_lo).
Axes of the slice: x: 4, y: 4, z: 16 (z_hi: 4, z_lo: 4; z = z_hi * 4 + z_lo), core: 2. Of those that a mesh axis runs over, the one named last changes fastest.
Arguments:
- x_block: bfloat16 [8, 131072], P(None, ('row', 'col')), may hold values from -6 to 6
- p_block: bfloat16 [8, 131072], P(None, ('row', 'col')), may hold values from -6 to 6
- tile_values: bfloat16 [24576, 128, 128], P(('row', 'col')), may hold values from -0.109375 to 0.109375
- tile_brow: int32 [24576], P(('row', 'col')), may hold values from 0 to 1023, as said below
- tile_bcol: int32 [24576], P(('row', 'col')), may hold values from 0 to 1023, as said below
- tile_count: int32 [512], P(('row', 'col')), may hold values from 1 to 48, as said below
Outputs:
- images: float32 [16, 131072], P(None, ('row', 'col'))
- projected: float32 [2, 16, 16], replicated
Inputs may be any that keep to these rules, and one draw needn't show every extreme that they name: Slot k belongs to device d = k // 48 with grid row r = d // 16 and column c = d % 16; tile_brow[k] // 2 lies in r * 16 to r * 16 + 15, and tile_bcol[k] <= tile_brow[k]. Repeated tiles add. tile_bcol[k] // 2 = c + 16 * m for some m, with c the column of the slot's device as above. `tile_count`: every device of the last grid row has 48 live slots.
All inputs are finite; a program needn't handle non-finite values.
Results may differ from a plain program's by a relative error of at most 0.0003.
Values may be sent and summed in bfloat16 or wider, within the bound.
A program may use at most 64 MiB of HBM per device.

v0:
```python
import jax
import jax.numpy as jnp
from jax import lax
from jax.sharding import PartitionSpec as P


def on_device(x_block, p_block, tile_values, tile_brow, tile_bcol, tile_count):
    row_size = lax.axis_size("row")
    col_size = lax.axis_size("col")
    row_pos = lax.axis_index("row")
    tile_len = tile_values.shape[1]
    slots = tile_values.shape[0]
    own_blocks = x_block.shape[1] // tile_len
    row_blocks = own_blocks * col_size
    col_blocks = own_blocks * row_size
    local_row = tile_brow - row_pos * row_blocks
    column_group = tile_bcol // own_blocks
    local_col = column_group // col_size * own_blocks + tile_bcol % own_blocks
    live = (jnp.arange(slots) < tile_count[0]).astype(jnp.float32)
    row_onehot = (local_row[:, None] == jnp.arange(row_blocks)[None, :]).astype(jnp.float32) * live[
        :, None
    ]
    col_onehot = (local_col[:, None] == jnp.arange(col_blocks)[None, :]).astype(jnp.float32) * live[
        :, None
    ]

    def multiply(vectors):
        width = vectors.shape[0]
        near = lax.all_gather(vectors, "col", axis=1, tiled=True).reshape(
            width, row_blocks, tile_len
        )
        far = lax.all_gather(vectors, "row", axis=1, tiled=True).reshape(
            width, col_blocks, tile_len
        )
        down = jnp.einsum(
            "kij,vkj->vki", tile_values, far[:, local_col], preferred_element_type=jnp.float32
        )
        across = jnp.einsum(
            "kij,vki->vkj", tile_values, near[:, local_row], preferred_element_type=jnp.float32
        )
        down_rows = jnp.einsum(
            "vki,kb->vbi", down, row_onehot, precision=lax.Precision.HIGHEST
        ).reshape(width, row_blocks * tile_len)
        across_rows = jnp.einsum(
            "vkj,kb->vbj", across, col_onehot, precision=lax.Precision.HIGHEST
        ).reshape(width, col_blocks * tile_len)
        row_part = lax.psum_scatter(down_rows, "col", scatter_dimension=1, tiled=True)
        col_part = lax.psum_scatter(across_rows, "row", scatter_dimension=1, tiled=True)
        summed = row_part + col_part
        near_flat = near.reshape(width, row_blocks * tile_len)
        far_flat = far.reshape(width, col_blocks * tile_len)
        return (summed, down_rows, across_rows, near_flat, far_flat)

    first = multiply(x_block)
    second = multiply(p_block)
    images = jnp.concatenate([first[0], second[0]], axis=0)
    down_rows = jnp.concatenate([first[1], second[1]], axis=0)
    across_rows = jnp.concatenate([first[2], second[2]], axis=0)
    near_flat = jnp.concatenate([first[3], second[3]], axis=0)
    far_flat = jnp.concatenate([first[4], second[4]], axis=0)
    stacked_half = jnp.concatenate([x_block, p_block], axis=0)
    correlation = jnp.dot(stacked_half, stacked_half.T, preferred_element_type=jnp.float32)
    hamilton = jnp.dot(stacked_half.astype(jnp.float32), images.T, precision=lax.Precision.HIGHEST)
    hamilton, correlation = lax.psum((hamilton, correlation), ("row", "col"))
    order = x_block.shape[1] * row_size * col_size
    return (images, jnp.stack([hamilton, correlation]) / order)


def solution(mesh):
    return jax.shard_map(
        on_device,
        mesh=mesh,
        in_specs=(
            P(None, ("row", "col")),
            P(None, ("row", "col")),
            P(("row", "col"), None, None),
            P(("row", "col")),
            P(("row", "col")),
            P(("row", "col")),
        ),
        out_specs=(P(None, ("row", "col")), P()),
        check_vma=False,
    )
```

profile of v0, /device:TPU:1, one launch (start us, length us, event | category | flops | bytes accessed | tf_op | source)
XLA Modules:
  0.0 569.9 jit_solution(14689217991121513722)
XLA Ops:
  7.2 0.0 copy-start
  7.2 0.0 copy-start.2
  7.2 0.0 reduce-scatter.5.cloned.1.call-start
  8.0 0.7 compare_select_fusion.1
  8.7 61.0 %all_gather.12 = bf16[8,8192]{1,0:T(8,128)(2,1)S(1)} all-gather(bf16[8,256]{1,0:T(8,128)(2,1)} %param.6), channel_id=1, replica_groups=mesh['row'=32,'col'=16] {'row'}, dimensions={1}, use_global_device_ids=true | all-gather | bytes 135168 | tf_op jit(solution)/shard_map/all_gather | solution.py:32
  69.7 0.7 compare_select_fusion
  70.3 0.6 gather_fusion
  71.0 0.0 copy-done
  71.0 0.9 fusion.14
  71.9 0.3 convolution_bitcast_fusion.3
  72.2 0.7 copy.39
  72.9 0.0 reduce-scatter.5.cloned.1.call-update
  72.9 0.0 reduce-scatter.7.cloned.1.call-start
  73.0 0.0 copy-done.2
  73.0 34.9 %all_gather.13 = bf16[8,4096]{1,0:T(8,128)(2,1)S(1)} all-gather(bf16[8,256]{1,0:T(8,128)(2,1)S(1)} %copy-done.2), channel_id=1, replica_groups=mesh['row'=32,'col'=16] {'col'}, dimensions={1}, use_global_device_ids=true | all-gather | bytes 69632 | tf_op jit(solution)/shard_map/all_gather | solution.py:29
  108.0 0.6 gather_fusion.1
  108.6 0.0 copy-start.3
  108.6 0.5 fusion.12
  109.1 0.5 convolution_bitcast_fusion.1
  109.6 0.9 copy.37
  110.4 0.0 reduce-scatter.7.cloned.1.call-update
  110.5 0.0 reduce-scatter.9.cloned.1.call-start
  110.5 0.0 copy-done.3
  110.5 54.4 %all_gather.14 = bf16[8,8192]{1,0:T(8,128)(2,1)S(1)} all-gather(bf16[8,256]{1,0:T(8,128)(2,1)S(1)} %copy-done.3), channel_id=1, replica_groups=mesh['row'=32,'col'=16] {'row'}, dimensions={1}, use_global_device_ids=true | all-gather | bytes 135168 | tf_op jit(solution)/shard_map/all_gather | solution.py:32
  164.9 0.6 gather_fusion.2
  165.5 0.9 fusion.10
  166.4 0.3 convolution_bitcast_fusion.2
  166.7 0.7 copy.38
  167.4 0.0 reduce-scatter.9.cloned.1.call-update
  167.5 0.0 reduce-scatter.11.cloned.1.call-start
  167.5 30.3 %all_gather.15 = bf16[8,4096]{1,0:T(8,128)(2,1)S(1)} all-gather(bf16[8,256]{1,0:T(8,128)(2,1)S(1)} %copy-done.3), channel_id=1, replica_groups=mesh['row'=32,'col'=16] {'col'}, dimensions={1}, use_global_device_ids=true | all-gather | bytes 69632 | tf_op jit(solution)/shard_map/all_gather | solution.py:29
  197.8 0.6 gather_fusion.3
  198.4 0.5 fusion.8
  198.9 0.5 convolution_bitcast_fusion
  199.4 0.8 copy.36
  200.3 0.0 reduce-scatter.11.cloned.1.call-update
  200.3 0.1 convolution_bitcast_fusion.4
  200.4 0.0 reduce-scatter.5.cloned.1.call-done
  200.4 62.3 %reduce-scatter.7.cloned.1.call-done = f32[8,256]{1,0:T(8,128)} async-done(((f32[8,8192]{1,0:T(8,128)}), f32[8,256]{1,0:T(8,128)}) %reduce-scatter.7.cloned.1.call-update) | async-done | bytes 8208 | tf_op jit(solution)/shard_map/reduce_scatter | solution.py:48
  262.8 0.7 add.41
  263.5 75.2 %reduce-scatter.9.cloned.1.call-done = f32[8,256]{1,0:T(8,128)} async-done(((f32[8,4096]{1,0:T(8,128)}), f32[8,256]{1,0:T(8,128)}) %reduce-scatter.9.cloned.1.call-update) | async-done | bytes 8208 | tf_op jit(solution)/shard_map/reduce_scatter | solution.py:47
  338.7 121.2 %reduce-scatter.11.cloned.1.call-done = f32[8,256]{1,0:T(8,128)} async-done(((f32[8,8192]{1,0:T(8,128)}), f32[8,256]{1,0:T(8,128)}) %reduce-scatter.11.cloned.1.call-update) | async-done | bytes 8208 | tf_op jit(solution)/shard_map/reduce_scatter | solution.py:48
  460.0 0.7 add.42
  460.7 0.0 copy-start.1
  460.7 0.1 convolution_bitcast_fusion.5
  460.8 102.0 %all-reduce = (f32[1,16,16]{2,1,0:T(8,128)S(1)}, f32[1,16,16]{2,1,0:T(8,128)S(1)}) all-reduce(f32[1,16,16]{2,1,0:T(8,128)S(1)} %convolution_bitcast_fusion.4, f32[1,16,16]{2,1,0:T(8,128)S(1)} %convolution_bitcast_fusion.5), channel_id=1, replica_groups=mesh['row'=32,'col'=16] {'row','col'}, use_global_device_ids=true, to_apply=%region_5.6 | all-reduce | flops 512 | bytes 4096 | tf_op jit(solution)/shard_map/psum | solution.py:64
  562.8 0.6 maximum_multiply_fusion
  563.4 0.0 copy-done.1
  (6 shorter events, 0.0 us)
Async XLA Ops:
  7.2 63.8 %copy-start = (bf16[48,128,128]{2,1,0:T(8,128)(2,1)S(1)}, bf16[48,128,128]{2,1,0:T(8,128)(2,1)}, u32[]{:S(2)}) copy-start(bf16[48,128,128]{2,1,0:T(8,128)(2,1)} %param.8) | copy-start | bytes 4718596
  7.2 65.8 %copy-start.2 = (bf16[8,256]{1,0:T(8,128)(2,1)S(1)}, bf16[8,256]{1,0:T(8,128)(2,1)}, u32[]{:S(2)}) copy-start(bf16[8,256]{1,0:T(8,128)(2,1)} %param.6) | copy-start | bytes 12292
  7.2 193.2 %reduce-scatter.5.cloned.1.call-start = ((), (), s32[]{:S(2)}) async-start(), calls=%async_computation.4 | async-start | bytes 139264 | tf_op jit(solution)/shard_map/reduce_scatter | solution.py:47
  72.9 189.8 %reduce-scatter.7.cloned.1.call-start = ((), (), s32[]{:S(2)}) async-start(), calls=%async_computation.5 | async-start | bytes 270336 | tf_op jit(solution)/shard_map/reduce_scatter | solution.py:48
  108.6 2.0 copy-start.3
  110.5 228.3 %reduce-scatter.9.cloned.1.call-start = ((), (), s32[]{:S(2)}) async-start(), calls=%async_computation.6 | async-start | bytes 139264 | tf_op jit(solution)/shard_map/reduce_scatter | solution.py:47
  167.5 292.5 %reduce-scatter.11.cloned.1.call-start = ((), (), s32[]{:S(2)}) async-start(), calls=%async_computation.7 | async-start | bytes 270336 | tf_op jit(solution)/shard_map/reduce_scatter | solution.py:48
  460.7 102.7 %copy-start.1 = (f32[16,256]{1,0:T(8,128)}, f32[16,256]{1,0:T(8,128)S(1)}, u32[]{:S(2)}) copy-start(f32[16,256]{1,0:T(8,128)S(1)} %pad_maximum_fusion) | copy-start | bytes 49156
Sparse Core Ops, SparseCore 0:
  73.1 68.2 reduce-scatter.4
  146.3 116.4 reduce-scatter.6
  265.8 72.8 reduce-scatter.8
  342.9 117.0 reduce-scatter.10
where the time goes:
time: 570 us
  blocking collectives  283 us (50%)
  waiting for transfers between devices  259 us (45%)
  between operations  14.6 us (3%)
    reduce_scatter x2, waiting for transfers between devices, multiply(): lax.psum_scatter(across_rows, 'row', scatter_dimension=1, tiled=True)  184 us
    all_gather x2, blocking collectives, multiply(): lax.all_gather(vectors, 'row', axis=1, tiled=True)  115 us
    psum x1, blocking collectives, on_device(): hamilton, correlation = lax.psum((hamilton, correlation), ('row', 'col'))  102 us
    reduce_scatter x2, waiting for transfers between devices, multiply(): lax.psum_scatter(down_rows, 'col', scatter_dimension=1, tiled=True)  75.2 us
    all_gather x2, blocking collectives, multiply(): lax.all_gather(vectors, 'col', axis=1, tiled=True)  65.2 us
  transfers between devices with their start and end apart: 4, of which 3 were waited for; matrix products, arithmetic and copies ran while one was open for 1% of the time, Pallas kernels for 0%

commit v1 on v0

v1 whole, which is shorter than its diff:
```python
import functools

import jax
import jax.numpy as jnp
from jax import lax
from jax.experimental import pallas as pl
from jax.experimental.pallas import tpu as pltpu
from jax.sharding import PartitionSpec as P

MESH = pl.DeviceIdType.MESH
F32 = jnp.float32
BF16 = jnp.bfloat16
VB = 16
TL = 128
NT = (((1,), (1,)), ((), ()))
NN = (((1,), (0,)), ((), ()))


def iota(shape, dim):
    return lax.broadcasted_iota(jnp.int32, shape, dim)


def split_dot(value, dims, other):
    return lax.dot_general(
        value, other, dims, precision=lax.Precision.HIGHEST, preferred_element_type=F32
    )


def fold_small(small):
    spread = (iota((VB, TL), 1) % VB == iota((VB, TL), 0)).astype(F32)
    wide = split_dot(small, NN, spread)
    keep = iota((VB, TL), 1) // VB == iota((VB, TL), 0) % 8
    wide = jnp.where(keep, wide, 0.0)
    top = jnp.sum(wide[0:8], axis=0, keepdims=True)
    low = jnp.sum(wide[8:16], axis=0, keepdims=True)
    return top, low


def unfold_small(top, low):
    keep = iota((VB, TL), 1) // VB == iota((VB, TL), 0) % 8
    upper = iota((VB, TL), 0) < 8
    wide = jnp.where(upper, jnp.broadcast_to(top, (VB, TL)), jnp.broadcast_to(low, (VB, TL)))
    wide = jnp.where(keep, wide, 0.0)
    gather = (iota((TL, VB), 0) % VB == iota((TL, VB), 1)).astype(F32)
    return split_dot(wide, NN, gather)


def kernel(
    slots,
    x_ref,
    p_ref,
    tiles_hbm,
    brow_s,
    bcol_s,
    brow_v,
    bcol_v,
    count_s,
    images_ref,
    small_ref,
    tiles,
    near,
    far,
    kron_row,
    kron_col,
    pieces,
    down_rows,
    across_rows,
    core_in,
    x_in,
    zh_in,
    y_in,
    zl_in,
    gram,
    z_small,
    xy_small,
    core_small,
    tile_sem,
    s_near,
    r_near,
    s_far,
    r_far,
    s_row,
    r_row,
    s_col,
    r_col,
    s_small,
    r_small,
):
    row, col = lax.axis_index("row"), lax.axis_index("col")
    x, zh, core = row // 8, (row // 2) % 4, row % 2
    y, zl = col // 4, col % 4

    def peer(dx=0, dy=0, dzh=0, dzl=0, dc=0):
        return (
            ((x + dx) % 4) * 8 + ((zh + dzh) % 4) * 2 + (core + dc) % 2,
            ((y + dy) % 4) * 4 + (zl + dzl) % 4,
        )

    def copy(src, dst, send, recv, to):
        return pltpu.make_async_remote_copy(
            src_ref=src, dst_ref=dst, send_sem=send, recv_sem=recv, device_id=to, device_id_type=MESH
        )

    def start(src, dst, send, recv, to):
        desc = copy(src, dst, send, recv, to)
        desc.start()
        return desc

    load = pltpu.make_async_copy(tiles_hbm, tiles, tile_sem)
    load.start()
    barrier = pltpu.get_barrier_semaphore()
    friends = (
        [peer(dzl=i) for i in (1, 2, 3)]
        + [peer(dy=i) for i in (1, 2, 3)]
        + [peer(dx=i) for i in (1, 2, 3)]
        + [peer(dzh=1), peer(dzh=3), peer(dc=1)]
    )
    for to in friends:
        pl.semaphore_signal(barrier, inc=1, device_id=to, device_id_type=MESH)

    for b in range(2):
        own = jnp.concatenate(
            [x_ref[:, b * TL : (b + 1) * TL].astype(F32), p_ref[:, b * TL : (b + 1) * TL].astype(F32)],
            axis=0,
        ).astype(BF16)
        near[b] = own
        far[b] = own

    def place(rel):
        lane = iota((8, slots), 1)
        rel = jnp.where(lane < count_s[0], jnp.broadcast_to(rel, (8, slots)), 255)
        spread = (iota((slots, slots * VB), 1) // VB == iota((slots, slots * VB), 0)).astype(BF16)
        wide = lax.dot_general(rel.astype(F32).astype(BF16), spread, NN, preferred_element_type=F32)
        wide = jnp.concatenate([wide, wide], axis=0)
        diag = iota((VB, slots * VB), 1) % VB == iota((VB, slots * VB), 0)
        return jnp.where(diag, wide, 255.0)

    def near_index(brow):
        c = (brow // 2) % 16
        return (((c // 4 - y) & 3) * 4 + ((c % 4 - zl) & 3)) * 2 + brow % 2

    def far_index(bcol):
        m = bcol // 32
        return (
            ((((m % 2) ^ core) * 4 + ((m // 8 - x) & 3)) * 4 + (((m // 2) % 4 - zh) & 3)) * 2 + bcol % 2
        )

    place_row = place(near_index(brow_v[...]))
    place_col = place(far_index(bcol_v[...]))

    def build(ref, placed, b):
        ref[pl.ds(pl.multiple_of(b * VB, VB), VB), :] = jnp.where(
            placed == b.astype(F32), 1.0, 0.0
        ).astype(BF16)

    @pl.loop(0, 64)
    def _(b):
        build(kron_col, place_col, b)

    @pl.loop(0, 32)
    def _(b):
        build(kron_row, place_row, b)

    pl.semaphore_wait(barrier, len(friends))
    sent = []

    near_zl = []
    for i in (3, 2, 1):
        near_zl.append(
            start(near.at[pl.ds(0, 2)], near.at[pl.ds((4 - i) * 2, 2)], s_near.at[i], r_near.at[i], peer(dzl=i))
        )
    far_up = start(far.at[pl.ds(0, 2)], far.at[pl.ds(6, 2)], s_far.at[0], r_far.at[0], peer(dzh=1))
    far_dn = start(far.at[pl.ds(0, 2)], far.at[pl.ds(2, 2)], s_far.at[1], r_far.at[1], peer(dzh=3))
    sent += near_zl + [far_up, far_dn]
    for d in near_zl:
        d.wait_recv()
    near_y = []
    for i in (2, 1, 3):
        near_y.append(
            start(
                near.at[pl.ds(0, 8)], near.at[pl.ds((4 - i) * 8, 8)], s_near.at[3 + i], r_near.at[3 + i], peer(dy=i)
            )
        )
    sent += near_y
    far_up.wait_recv()
    far_two = start(far.at[pl.ds(6, 2)], far.at[pl.ds(4, 2)], s_far.at[2], r_far.at[2], peer(dzh=1))
    far_dn.wait_recv()
    sent.append(far_two)
    for d in near_y:
        d.wait_recv()
    load.wait()

    def multiply(vec_ref, index_of, index_s, dims):
        @pl.loop(0, slots // 8)
        def _(step):
            for j in range(8):
                k = step * 8 + j
                vec = vec_ref[index_of(index_s[k])]
                part = lax.dot_general(vec, tiles[k], dims, preferred_element_type=F32)
                high = part.astype(BF16)
                rows = pl.ds(pl.multiple_of(k * VB, VB), VB)
                pieces[rows, 0:TL] = high
                pieces[rows, TL : 2 * TL] = (part - high.astype(F32)).astype(BF16)

    def scatter(kron, first, blocks, out_ref):
        both = lax.dot_general(
            kron[first * VB : (first + blocks) * VB, :], pieces[...], NN, preferred_element_type=F32
        )
        out_ref[first : first + blocks] = (both[:, 0:TL] + both[:, TL : 2 * TL]).reshape(blocks, VB, TL)

    multiply(near, near_index, brow_s, NN)
    for part in range(4):
        scatter(kron_col, 32 + part * 8, 8, across_rows)
    core_rs = start(across_rows.at[pl.ds(32, 32)], core_in, s_row.at[0], r_row.at[0], peer(dc=1))
    for part in range(4):
        scatter(kron_col, part * 8, 8, across_rows)
    far_two.wait_recv()
    far_x = []
    for i in (2, 1, 3):
        far_x.append(
            start(far.at[pl.ds(0, 8)], far.at[pl.ds((4 - i) * 8, 8)], s_far.at[2 + i], r_far.at[2 + i], peer(dx=i))
        )
    core_rs.wait_recv()
    x_rs = []
    for i in (2, 1, 3):
        across_rows[i * 8 : i * 8 + 8] += core_in[i * 8 : i * 8 + 8]
        x_rs.append(
            start(across_rows.at[pl.ds(i * 8, 8)], x_in.at[pl.ds((i - 1) * 8, 8)], s_row.at[i], r_row.at[i], peer(dx=i))
        )
    across_rows[0:8] += core_in[0:8]
    sent += [core_rs] + far_x + x_rs

    for d in far_x:
        d.wait_recv()
    far_core = start(far.at[pl.ds(0, 32)], far.at[pl.ds(32, 32)], s_far.at[6], r_far.at[6], peer(dc=1))
    sent.append(far_core)

    def hamilton_step(b, total):
        rows = across_rows[b]
        high = rows.astype(BF16)
        low = (rows - high.astype(F32)).astype(BF16)
        return (
            total
            + lax.dot_general(high, far[b], NT, preferred_element_type=F32)
            + lax.dot_general(low, far[b], NT, preferred_element_type=F32)
        )

    half = lax.fori_loop(0, 32, hamilton_step, jnp.zeros((VB, VB), F32), unroll=4)
    correlation = lax.dot_general(near[0], near[0], NT, preferred_element_type=F32) + lax.dot_general(
        near[1], near[1], NT, preferred_element_type=F32
    )
    h_top, h_low = fold_small(half)
    c_top, c_low = fold_small(correlation)
    gram[0, 0:1] = h_top
    gram[0, 1:2] = h_low
    gram[0, 2:3] = c_top
    gram[0, 3:4] = c_low
    small_z = []
    for n in range(1, 16):
        zz = zh * 4 + zl + n
        to = (x * 8 + ((zz // 4) % 4) * 2 + core, y * 4 + zz % 4)
        small_z.append(start(gram.at[0], z_small.at[n - 1], s_small.at[n - 1], r_small.at[n - 1], to))
    sent += small_z

    far_core.wait_recv()
    multiply(far, far_index, bcol_s, NT)
    y_rs = []
    for i in (2, 1, 3, 0):
        scatter(kron_row, i * 8, 8, down_rows)
        if i:
            y_rs.append(
                start(
                    down_rows.at[pl.ds(i * 8, 8)], y_in.at[pl.ds((i - 1) * 8, 8)], s_col.at[i], r_col.at[i], peer(dy=i)
                )
            )
    sent += y_rs

    for d in x_rs:
        d.wait_recv()
    zh_rs = []
    for i in (2, 1, 3, 0):
        mine = pl.ds(i * 2, 2)
        across_rows[mine] += x_in[i * 2 : i * 2 + 2] + x_in[8 + i * 2 : 10 + i * 2] + x_in[16 + i * 2 : 18 + i * 2]
        if i:
            zh_rs.append(
                start(across_rows.at[mine], zh_in.at[pl.ds((i - 1) * 2, 2)], s_row.at[3 + i], r_row.at[3 + i], peer(dzh=i))
            )
    sent += zh_rs

    for d in y_rs:
        d.wait_recv()
    zl_rs = []
    for i in (3, 2, 1, 0):
        mine = pl.ds(i * 2, 2)
        down_rows[mine] += y_in[i * 2 : i * 2 + 2] + y_in[8 + i * 2 : 10 + i * 2] + y_in[16 + i * 2 : 18 + i * 2]
        if i:
            zl_rs.append(
                start(down_rows.at[mine], zl_in.at[pl.ds((i - 1) * 2, 2)], s_col.at[3 + i], r_col.at[3 + i], peer(dzl=i))
            )
    sent += zl_rs

    for d in small_z:
        d.wait_recv()
    gram[1] = gram[0] + jnp.sum(z_small[...], axis=0)
    small_xy = []
    for n in range(1, 16):
        to = peer(dx=n // 4, dy=n % 4)
        small_xy.append(start(gram.at[1], xy_small.at[n - 1], s_small.at[14 + n], r_small.at[14 + n], to))
    sent += small_xy

    for d in zl_rs + zh_rs:
        d.wait_recv()
    for b in range(2):
        images_ref[:, b * TL : (b + 1) * TL] = (
            (down_rows[b] + across_rows[b])
            + ((zl_in[b] + zl_in[2 + b] + zl_in[4 + b]) + (zh_in[b] + zh_in[2 + b] + zh_in[4 + b]))
        )

    for d in small_xy:
        d.wait_recv()
    gram[2] = gram[1] + jnp.sum(xy_small[...], axis=0)
    small_core = start(gram.at[2], core_small, s_small.at[30], r_small.at[30], peer(dc=1))
    sent.append(small_core)
    small_core.wait_recv()
    scale = 1.0 / (512 * 256)
    whole = (gram[2] + core_small[...]) * scale
    part = unfold_small(whole[0:1], whole[1:2])
    eye = (iota((VB, VB), 0) == iota((VB, VB), 1)).astype(F32)
    small_ref[0] = part + lax.dot_general(
        eye, part, NT, precision=lax.Precision.HIGHEST, preferred_element_type=F32
    )
    small_ref[1] = unfold_small(whole[2:3], whole[3:4])
    for d in sent:
        d.wait_send()


def on_device(x_block, p_block, tile_values, tile_brow, tile_bcol, tile_count):
    slots = tile_values.shape[0]
    vmem = pl.BlockSpec(memory_space=pltpu.VMEM)
    smem = pl.BlockSpec(memory_space=pltpu.SMEM)
    dma = pltpu.SemaphoreType.DMA
    return pl.pallas_call(
        functools.partial(kernel, slots),
        out_shape=(
            jax.ShapeDtypeStruct((VB, 2 * TL), F32),
            jax.ShapeDtypeStruct((2, VB, VB), F32),
        ),
        in_specs=[vmem, vmem, pl.BlockSpec(memory_space=pl.ANY), smem, smem, vmem, vmem, smem],
        out_specs=(vmem, vmem),
        scratch_shapes=[
            pltpu.VMEM((slots, TL, TL), BF16),
            pltpu.VMEM((32, VB, TL), BF16),
            pltpu.VMEM((64, VB, TL), BF16),
            pltpu.VMEM((32 * VB, slots * VB), BF16),
            pltpu.VMEM((64 * VB, slots * VB), BF16),
            pltpu.VMEM((slots * VB, 2 * TL), BF16),
            pltpu.VMEM((32, VB, TL), F32),
            pltpu.VMEM((64, VB, TL), F32),
            pltpu.VMEM((32, VB, TL), F32),
            pltpu.VMEM((24, VB, TL), F32),
            pltpu.VMEM((6, VB, TL), F32),
            pltpu.VMEM((24, VB, TL), F32),
            pltpu.VMEM((6, VB, TL), F32),
            pltpu.VMEM((3, 4, TL), F32),
            pltpu.VMEM((15, 4, TL), F32),
            pltpu.VMEM((15, 4, TL), F32),
            pltpu.VMEM((4, TL), F32),
            dma,
            dma((7,)),
            dma((7,)),
            dma((7,)),
            dma((7,)),
            dma((7,)),
            dma((7,)),
            dma((7,)),
            dma((7,)),
            dma((31,)),
            dma((31,)),
        ],
        compiler_params=pltpu.CompilerParams(
            collective_id=0, has_side_effects=True, vmem_limit_bytes=32 * 2**20
        ),
    )(
        x_block,
        p_block,
        tile_values,
        tile_brow,
        tile_bcol,
        tile_brow.reshape(1, slots),
        tile_bcol.reshape(1, slots),
        tile_count,
    )


def solution(mesh):
    return jax.shard_map(
        on_device,
        mesh=mesh,
        in_specs=(
            P(None, ("row", "col")),
            P(None, ("row", "col")),
            P(("row", "col"), None, None),
            P(("row", "col")),
            P(("row", "col")),
            P(("row", "col")),
        ),
        out_specs=(P(None, ("row", "col")), P()),
        check_vma=False,
    )
```

time: 570 us -> 52.8 us (0.09)
  blocking collectives: 283 us -> 0 us
  waiting for transfers between devices: 259 us -> 0 us
  Pallas kernels: 0 us -> 46 us
  between operations: 14.6 us -> 1.3 us
    reduce_scatter x4 -> x0, waiting for transfers between devices: 259 us -> none  [the longest x2 184 us: multiply(): lax.psum_scatter(across_rows, 'row', scatter_dimension=1, tiled=True)]
    all_gather x4 -> x0, blocking collectives: 181 us -> none  [the longest x2 115 us: multiply(): lax.all_gather(vectors, 'row', axis=1, tiled=True)]
    psum x1 -> x0, blocking collectives: 102 us -> none  [on_device(): hamilton, correlation = lax.psum((hamilton, correlation), ('row', 'col'))]
    pallas_call x0 -> x1, Pallas kernels: none -> 46 us  [on_device(): pl.pallas_call(functools.partial(kernel, slots), out_shape=(jax.ShapeDtyp...]
  transfers between devices with their start and end apart: 4 -> 0, of which waited for: 3 -> 0; matrix products, arithmetic and copies ran while one was open for 1% -> 0% of each run, Pallas kernels for 0% -> 0%
where the time goes in v1:
time: 52.8 us; the launch traced here: 52.6 us
  Pallas kernels  46 us (87%)
  local copies, waits for them, and re-layouts  5.3 us (10%)
  between operations  1.3 us (2%)
    pallas_call x1, Pallas kernels, on_device(): pl.pallas_call(functools.partial(kernel, slots), out_shape=(jax.ShapeDtyp...  46 us
    unnamed x12, local copies, waits for them, and re-layouts  5.3 us

profile of v1, /device:TPU:1, one launch (start us, length us, event | category | flops | bytes accessed | tf_op | source)
XLA Modules:
  0.0 52.6 jit_solution(9526831213894989978)
XLA Ops:
  1.3 0.0 copy-start
  1.3 1.4 %copy-done = bf16[48,128,128]{2,1,0:T(8,128)(2,1)S(1)} copy-done((bf16[48,128,128]{2,1,0:T(8,128)(2,1)S(1)}, bf16[48,128,128]{2,1,0:T(8,128)(2,1)}, u32[]{:S(2)}) %copy-start) | copy-done | bytes 1572888
  2.7 0.0 copy-start.1
  2.7 0.7 %copy-done.1 = bf16[8,256]{1,0:T(8,128)(2,1)S(1)} copy-done((bf16[8,256]{1,0:T(8,128)(2,1)S(1)}, bf16[8,256]{1,0:T(8,128)(2,1)}, u32[]{:S(2)}) %copy-start.1) | copy-done | bytes 4120
  3.4 0.0 copy-start.2
  3.4 0.7 %copy-done.2 = bf16[8,256]{1,0:T(8,128)(2,1)S(1)} copy-done((bf16[8,256]{1,0:T(8,128)(2,1)S(1)}, bf16[8,256]{1,0:T(8,128)(2,1)}, u32[]{:S(2)}) %copy-start.2) | copy-done | bytes 4120
  4.1 0.0 copy-start.3
  4.1 0.7 %copy-done.3 = s32[48]{0:T(128)S(1)} copy-done((s32[48]{0:T(128)S(1)}, s32[48]{0:T(128)}, u32[]{:S(2)}) %copy-start.3) | copy-done | bytes 216
  4.7 0.0 copy-start.4
  4.7 0.7 %copy-done.4 = s32[48]{0:T(128)S(1)} copy-done((s32[48]{0:T(128)S(1)}, s32[48]{0:T(128)}, u32[]{:S(2)}) %copy-start.4) | copy-done | bytes 216
  5.4 46.0 %shard_map.77 = (f32[16,256]{1,0:T(8,128)S(1)}, f32[2,16,16]{2,1,0:T(8,128)S(1)}) custom-call(bf16[8,256]{1,0:T(8,128)(2,1)S(1)} %copy-done.1, bf16[8,256]{1,0:T(8,128)(2,1)S(1)} %copy-done.2, bf16[48,128,128]{2,1,0:T(8,128)(2,1)S(1)} %copy-done, s32[48]{0:T(128)S(1)} %copy-done.3, s32[48]{0:T(128)S(1)} %copy-done.4, s32[1,48]{1,0:T(1,128)S(1)} %bitcast.2, ...), custom_call_target="tpu_custom_call" | custom-call | tf_op jit(solution)/shard_map/pallas_call | solution.py:342
  51.4 0.6 %copy.11 = f32[16,256]{1,0:T(8,128)} copy(f32[16,256]{1,0:T(8,128)S(1)} %get-tuple-element.4) | data formatting | bytes 32768
  52.0 0.6 %copy.12 = f32[2,16,16]{2,1,0:T(8,128)} copy(f32[2,16,16]{2,1,0:T(8,128)S(1)} %get-tuple-element.5) | data formatting | bytes 4096
Async XLA Ops:
  1.3 1.4 %copy-start = (bf16[48,128,128]{2,1,0:T(8,128)(2,1)S(1)}, bf16[48,128,128]{2,1,0:T(8,128)(2,1)}, u32[]{:S(2)}) copy-start(bf16[48,128,128]{2,1,0:T(8,128)(2,1)} %tiles_hbm.1) | copy-start | bytes 4718596
  2.7 0.7 %copy-start.1 = (bf16[8,256]{1,0:T(8,128)(2,1)S(1)}, bf16[8,256]{1,0:T(8,128)(2,1)}, u32[]{:S(2)}) copy-start(bf16[8,256]{1,0:T(8,128)(2,1)} %x_ref.1) | copy-start | bytes 12292
  3.4 0.7 %copy-start.2 = (bf16[8,256]{1,0:T(8,128)(2,1)S(1)}, bf16[8,256]{1,0:T(8,128)(2,1)}, u32[]{:S(2)}) copy-start(bf16[8,256]{1,0:T(8,128)(2,1)} %p_ref.1) | copy-start | bytes 12292
  4.1 0.7 %copy-start.3 = (s32[48]{0:T(128)S(1)}, s32[48]{0:T(128)}, u32[]{:S(2)}) copy-start(s32[48]{0:T(128)} %brow_s.1) | copy-start | bytes 580
  4.7 0.7 %copy-start.4 = (s32[48]{0:T(128)S(1)}, s32[48]{0:T(128)}, u32[]{:S(2)}) copy-start(s32[48]{0:T(128)} %bcol_s.1) | copy-start | bytes 580

commit v2 on v1

v2 whole, which is shorter than its diff:
```python
import functools

import jax
import jax.numpy as jnp
from jax import lax
from jax.experimental import pallas as pl
from jax.experimental.pallas import tpu as pltpu
from jax.sharding import PartitionSpec as P

MESH = pl.DeviceIdType.MESH
F32 = jnp.float32
BF16 = jnp.bfloat16
VB = 16
TL = 128
NT = (((1,), (1,)), ((), ()))
NN = (((1,), (0,)), ((), ()))


def iota(shape, dim):
    return lax.broadcasted_iota(jnp.int32, shape, dim)


def wide_mask():
    return iota((VB, TL), 1) // VB == iota((VB, TL), 0) % 8


def eight(block):
    return jnp.concatenate([block] * 8, axis=0)


def fold_small(ref, slot, wide):
    wide = jnp.where(wide_mask(), wide, 0.0)
    ref[slot, 0:1] = jnp.sum(wide[0:8], axis=0, keepdims=True)
    ref[slot, 1:2] = jnp.sum(wide[8:16], axis=0, keepdims=True)


def unfold_small(rows):
    upper = iota((VB, TL), 0) < 8
    wide = jnp.where(upper, jnp.broadcast_to(rows[0:1], (VB, TL)), jnp.broadcast_to(rows[1:2], (VB, TL)))
    wide = jnp.where(wide_mask(), wide, 0.0)
    turned = jnp.sum(wide.T.reshape(8, VB, VB), axis=0)
    for shift in (64, 32, 16):
        wide = wide + pltpu.roll(wide, shift, 1)
    return wide[:, 0:VB], turned


def kernel(
    slots,
    x_hbm,
    p_hbm,
    tiles_hbm,
    brow_hbm,
    bcol_hbm,
    count_s,
    images_ref,
    small_ref,
    x_ref,
    p_ref,
    brow_s,
    bcol_s,
    brow_v,
    bcol_v,
    tiles,
    near,
    far,
    kron_row,
    kron_col,
    pieces,
    down_rows,
    across_rows,
    core_in,
    x_in,
    zh_in,
    y_in,
    zl_in,
    gram,
    z_small,
    xy_small,
    corr,
    corr_in,
    load_sem,
    s_near,
    r_near,
    s_near_y,
    r_near_y,
    s_far,
    r_far,
    s_far_x,
    r_far_x,
    s_row,
    r_row,
    s_col,
    r_col,
    s_small,
    r_small,
    s_corr,
    r_corr,
):
    row, col = lax.axis_index("row"), lax.axis_index("col")
    x, zh, core = row // 8, (row // 2) % 4, row % 2
    y, zl = col // 4, col % 4

    def peer(dx=0, dy=0, dzh=0, dzl=0, dc=0):
        return (
            ((x + dx) % 4) * 8 + ((zh + dzh) % 4) * 2 + (core + dc) % 2,
            ((y + dy) % 4) * 4 + (zl + dzl) % 4,
        )

    def copy(src, dst, send, recv, to):
        return pltpu.make_async_remote_copy(
            src_ref=src, dst_ref=dst, send_sem=send, recv_sem=recv, device_id=to, device_id_type=MESH
        )

    def start(src, dst, send, recv, to):
        desc = copy(src, dst, send, recv, to)
        desc.start()
        return desc

    barrier = pltpu.get_barrier_semaphore()
    friends = (
        [peer(dzl=i) for i in (1, 2, 3)]
        + [peer(dy=i) for i in (1, 2, 3)]
        + [peer(dx=i) for i in (1, 2, 3)]
        + [peer(dzh=1), peer(dzh=3), peer(dc=1)]
    )
    for to in friends:
        pl.semaphore_signal(barrier, inc=1, device_id=to, device_id_type=MESH)

    fetches = [
        pltpu.make_async_copy(src, dst, load_sem.at[n])
        for n, (src, dst) in enumerate(
            [
                (x_hbm, x_ref),
                (p_hbm, p_ref),
                (bcol_hbm, bcol_v),
                (brow_hbm, brow_v),
                (bcol_hbm.at[0], bcol_s),
                (brow_hbm.at[0], brow_s),
                (tiles_hbm, tiles),
            ]
        )
    ]
    for fetch in fetches:
        fetch.start()
    fetches[0].wait()
    fetches[1].wait()

    for b in range(2):
        own = jnp.concatenate(
            [x_ref[:, b * TL : (b + 1) * TL].astype(F32), p_ref[:, b * TL : (b + 1) * TL].astype(F32)],
            axis=0,
        ).astype(BF16)
        near[b] = own
        far[b] = own

    pl.semaphore_wait(barrier, len(friends))
    far_x = []

    def far_spread(slot):
        for i in (2, 1, 3):
            far_x.append(
                start(
                    far.at[pl.ds(slot * 2, 2)],
                    far.at[pl.ds((4 - i) * 8 + slot * 2, 2)],
                    s_far_x.at[slot * 3 + i - 1],
                    r_far_x.at[slot * 3 + i - 1],
                    peer(dx=i),
                )
            )

    far_up = start(far.at[pl.ds(0, 2)], far.at[pl.ds(6, 2)], s_far.at[0], r_far.at[0], peer(dzh=1))
    far_dn = start(far.at[pl.ds(0, 2)], far.at[pl.ds(2, 2)], s_far.at[1], r_far.at[1], peer(dzh=3))
    near_zl = []
    for i in (3, 2, 1):
        near_zl.append(
            start(near.at[pl.ds(0, 2)], near.at[pl.ds((4 - i) * 2, 2)], s_near.at[i], r_near.at[i], peer(dzl=i))
        )
    near_y = []

    def near_spread(slot):
        for i in (2, 1, 3):
            near_y.append(
                start(
                    near.at[pl.ds(slot * 2, 2)],
                    near.at[pl.ds((4 - i) * 8 + slot * 2, 2)],
                    s_near_y.at[slot * 3 + i - 1],
                    r_near_y.at[slot * 3 + i - 1],
                    peer(dy=i),
                )
            )

    near_spread(0)
    far_spread(0)

    def place(rel):
        lane = iota((8, slots), 1)
        rel = jnp.where(lane < count_s[0], jnp.broadcast_to(rel, (8, slots)), 255)
        spread = (iota((slots, slots * VB), 1) // VB == iota((slots, slots * VB), 0)).astype(BF16)
        wide = lax.dot_general(rel.astype(F32).astype(BF16), spread, NN, preferred_element_type=F32)
        wide = jnp.concatenate([wide, wide], axis=0)
        diag = iota((VB, slots * VB), 1) % VB == iota((VB, slots * VB), 0)
        return jnp.where(diag, wide, 255.0)

    def near_index(brow):
        c = (brow // 2) % 16
        return (((c // 4 - y) & 3) * 4 + ((c % 4 - zl) & 3)) * 2 + brow % 2

    def far_index(bcol):
        m = bcol // 32
        return (
            ((((m % 2) ^ core) * 4 + ((m // 8 - x) & 3)) * 4 + (((m // 2) % 4 - zh) & 3)) * 2 + bcol % 2
        )

    def build(ref, rel, blocks):
        placed = place(rel)

        @pl.loop(0, blocks // 8)
        def _(step):
            for j in range(8):
                b = step * 8 + j
                ref[pl.ds(pl.multiple_of(b * VB, VB), VB), :] = jnp.where(
                    placed == b.astype(F32), 1.0, 0.0
                ).astype(BF16)

    for fetch in fetches[2:6]:
        fetch.wait()
    build(kron_col, far_index(bcol_v[...]), 64)
    for d, slot in zip(near_zl[::-1], (3, 2, 1)):
        d.wait_recv()
        near_spread(slot)
    far_up.wait_recv()
    far_two = start(far.at[pl.ds(6, 2)], far.at[pl.ds(4, 2)], s_far.at[2], r_far.at[2], peer(dzh=1))
    far_spread(3)
    far_dn.wait_recv()
    far_spread(1)
    build(kron_row, near_index(brow_v[...]), 32)
    fetches[6].wait()
    for d in near_y:
        d.wait_recv()

    def multiply(vec_ref, index_of, index_s, dims):
        for k in range(slots):
            part = lax.dot_general(vec_ref[index_of(index_s[k])], tiles[k], dims, preferred_element_type=F32)
            high = part.astype(BF16)
            rows = slice(k * VB, (k + 1) * VB)
            pieces[rows, 0:TL] = high
            pieces[rows, TL : 2 * TL] = (part - high.astype(F32)).astype(BF16)

    def scatter(kron, first, blocks, out_ref):
        both = lax.dot_general(
            kron[first * VB : (first + blocks) * VB, :], pieces[...], NN, preferred_element_type=F32
        )
        out_ref[first : first + blocks] = (both[:, 0:TL] + both[:, TL : 2 * TL]).reshape(blocks, VB, TL)

    multiply(near, near_index, brow_s, NN)
    scatter(kron_col, 32, 32, across_rows)
    core_rs = start(across_rows.at[pl.ds(32, 32)], core_in, s_row.at[0], r_row.at[0], peer(dc=1))
    far_two.wait_recv()
    far_spread(2)
    scatter(kron_col, 0, 32, across_rows)
    core_rs.wait_recv()
    x_rs = []
    for i in (2, 1, 3, 0):
        across_rows[i * 8 : i * 8 + 8] += core_in[i * 8 : i * 8 + 8]
        if i:
            x_rs.append(
                start(
                    across_rows.at[pl.ds(i * 8, 8)],
                    x_in.at[pl.ds((i - 1) * 8, 8)],
                    s_row.at[i],
                    r_row.at[i],
                    peer(dx=i),
                )
            )

    def share(blocks):
        high = [across_rows[b].astype(BF16) for b in blocks]
        low = [(across_rows[b] - h.astype(F32)).astype(BF16) for b, h in zip(blocks, high)]
        both = jnp.concatenate([jnp.concatenate(part, axis=1) for part in (high, low)], axis=0)
        vecs = jnp.concatenate([eight(far[b]) for b in blocks], axis=1)
        both = lax.dot_general(both, vecs, NT, preferred_element_type=F32)
        return both[0:VB] + both[VB : 2 * VB]

    for d in far_x[:9]:
        d.wait_recv()
    half = share([b for b in range(32) if b % 8 // 2 != 2])
    for d in far_x[9:]:
        d.wait_recv()
    half = half + share([b for b in range(32) if b % 8 // 2 == 2])
    far_core = start(far.at[pl.ds(0, 32)], far.at[pl.ds(32, 32)], s_far.at[6], r_far.at[6], peer(dc=1))
    fold_small(gram, 0, half)
    small_z = []
    for n in range(1, 16):
        zz = zh * 4 + zl + n
        to = (x * 8 + ((zz // 4) % 4) * 2 + core, y * 4 + zz % 4)
        small_z.append(start(gram.at[0], z_small.at[n - 1], s_small.at[n - 1], r_small.at[n - 1], to))

    far_core.wait_recv()
    multiply(far, far_index, bcol_s, NT)
    scatter(kron_row, 8, 24, down_rows)
    y_rs = []
    for i in (2, 1, 3):
        y_rs.append(
            start(
                down_rows.at[pl.ds(i * 8, 8)], y_in.at[pl.ds((i - 1) * 8, 8)], s_col.at[i], r_col.at[i], peer(dy=i)
            )
        )
    scatter(kron_row, 0, 8, down_rows)
    wide = jnp.concatenate([near[b] for b in range(32)], axis=1)
    tall = jnp.concatenate([eight(near[b]) for b in range(32)], axis=1)
    fold_small(corr, 0, lax.dot_general(wide, tall, NT, preferred_element_type=F32))
    corr_core = start(corr.at[0], corr_in.at[0], s_corr.at[0], r_corr.at[0], peer(dc=1))
    for d in x_rs:
        d.wait_recv()
    zh_rs = []
    for i in (2, 1, 3, 0):
        mine = pl.ds(i * 2, 2)
        across_rows[mine] += x_in[i * 2 : i * 2 + 2] + x_in[8 + i * 2 : 10 + i * 2] + x_in[16 + i * 2 : 18 + i * 2]
        if i:
            zh_rs.append(
                start(across_rows.at[mine], zh_in.at[pl.ds((i - 1) * 2, 2)], s_row.at[3 + i], r_row.at[3 + i], peer(dzh=i))
            )
    corr_core.wait_recv()
    corr[1] = corr[0] + corr_in[0]
    corr_x = [start(corr.at[1], corr_in.at[i], s_corr.at[i], r_corr.at[i], peer(dx=i)) for i in (1, 2, 3)]

    for d in y_rs:
        d.wait_recv()
    zl_rs = []
    for i in (3, 2, 1, 0):
        mine = pl.ds(i * 2, 2)
        down_rows[mine] += y_in[i * 2 : i * 2 + 2] + y_in[8 + i * 2 : 10 + i * 2] + y_in[16 + i * 2 : 18 + i * 2]
        if i:
            zl_rs.append(
                start(down_rows.at[mine], zl_in.at[pl.ds((i - 1) * 2, 2)], s_col.at[3 + i], r_col.at[3 + i], peer(dzl=i))
            )

    for d in corr_x:
        d.wait_recv()
    corr[2] = corr[1] + (corr_in[1] + corr_in[2] + corr_in[3])
    corr_zh = [start(corr.at[2], corr_in.at[3 + i], s_corr.at[3 + i], r_corr.at[3 + i], peer(dzh=i)) for i in (1, 2, 3)]

    for d in small_z:
        d.wait_recv()
    gram[1] = gram[0] + jnp.sum(z_small[...], axis=0)
    small_xy = []
    for n in (20, 21, 4, 5, 16, 17, 12, 13, 18, 19, 22, 23, 28, 29, 2, 3, 6, 7, 8, 9, 24, 25, 10, 11, 14, 15, 26, 27, 30, 31, 1):
        to = peer(dx=n // 8, dy=(n // 2) % 4, dc=n % 2)
        small_xy.append(start(gram.at[1], xy_small.at[n - 1], s_small.at[14 + n], r_small.at[14 + n], to))

    scale = 1.0 / (1024 * TL)
    for d in zl_rs + zh_rs + corr_zh:
        d.wait_recv()
    for b in range(2):
        images_ref[:, b * TL : (b + 1) * TL] = (
            (down_rows[b] + across_rows[b])
            + ((zl_in[b] + zl_in[2 + b] + zl_in[4 + b]) + (zh_in[b] + zh_in[2 + b] + zh_in[4 + b]))
        )
    small_ref[1] = unfold_small((corr[2] + (corr_in[4] + corr_in[5] + corr_in[6])) * scale)[0]

    for d in (
        [far_up, far_dn, far_two, far_core, core_rs, corr_core]
        + near_zl + near_y + far_x + x_rs + zh_rs + y_rs + zl_rs + corr_x + corr_zh + small_z
    ):
        d.wait_send()
    for d in small_xy:
        d.wait_recv()
    straight, turned = unfold_small((gram[1] + jnp.sum(xy_small[...], axis=0)) * scale)
    small_ref[0] = straight + turned
    for d in small_xy:
        d.wait_send()


def on_device(x_block, p_block, tile_values, tile_brow, tile_bcol, tile_count):
    slots = tile_values.shape[0]
    vmem = pl.BlockSpec(memory_space=pltpu.VMEM)
    dma = pltpu.SemaphoreType.DMA
    return pl.pallas_call(
        functools.partial(kernel, slots),
        out_shape=(
            jax.ShapeDtypeStruct((VB, 2 * TL), F32),
            jax.ShapeDtypeStruct((2, VB, VB), F32),
        ),
        in_specs=[pl.BlockSpec(memory_space=pltpu.HBM)] * 5 + [pl.BlockSpec(memory_space=pltpu.SMEM)],
        out_specs=(vmem, vmem),
        scratch_shapes=[
            pltpu.VMEM((8, 2 * TL), BF16),
            pltpu.VMEM((8, 2 * TL), BF16),
            pltpu.SMEM((slots,), jnp.int32),
            pltpu.SMEM((slots,), jnp.int32),
            pltpu.VMEM((1, slots), jnp.int32),
            pltpu.VMEM((1, slots), jnp.int32),
            pltpu.VMEM((slots, TL, TL), BF16),
            pltpu.VMEM((32, VB, TL), BF16),
            pltpu.VMEM((64, VB, TL), BF16),
            pltpu.VMEM((32 * VB, slots * VB), BF16),
            pltpu.VMEM((64 * VB, slots * VB), BF16),
            pltpu.VMEM((slots * VB, 2 * TL), BF16),
            pltpu.VMEM((32, VB, TL), F32),
            pltpu.VMEM((64, VB, TL), F32),
            pltpu.VMEM((32, VB, TL), F32),
            pltpu.VMEM((24, VB, TL), F32),
            pltpu.VMEM((6, VB, TL), F32),
            pltpu.VMEM((24, VB, TL), F32),
            pltpu.VMEM((6, VB, TL), F32),
            pltpu.VMEM((2, 2, TL), F32),
            pltpu.VMEM((15, 2, TL), F32),
            pltpu.VMEM((31, 2, TL), F32),
            pltpu.VMEM((3, 2, TL), F32),
            pltpu.VMEM((7, 2, TL), F32),
            dma((7,)),
            dma((4,)),
            dma((4,)),
            dma((12,)),
            dma((12,)),
            dma((7,)),
            dma((7,)),
            dma((12,)),
            dma((12,)),
            dma((7,)),
            dma((7,)),
            dma((7,)),
            dma((7,)),
            dma((46,)),
            dma((46,)),
            dma((7,)),
            dma((7,)),
        ],
        compiler_params=pltpu.CompilerParams(
            collective_id=0, has_side_effects=True, vmem_limit_bytes=32 * 2**20
        ),
    )(
        *(
            pltpu.with_memory_space_constraint(arg, pltpu.HBM)
            for arg in (
                x_block,
                p_block,
                tile_values,
                tile_brow.reshape(1, slots),
                tile_bcol.reshape(1, slots),
            )
        ),
        tile_count,
    )


def solution(mesh):
    return jax.shard_map(
        on_device,
        mesh=mesh,
        in_specs=(
            P(None, ("row", "col")),
            P(None, ("row", "col")),
            P(("row", "col"), None, None),
            P(("row", "col")),
            P(("row", "col")),
            P(("row", "col")),
        ),
        out_specs=(P(None, ("row", "col")), P()),
        check_vma=False,
    )
```

time: 52.8 us -> 48.1 us (0.911)
  local copies, waits for them, and re-layouts: 5.3 us -> 1.21 us
    unnamed x12 -> x2, local copies, waits for them, and re-layouts: 5.3 us -> 1.21 us
where the time goes in v2:
time: 48.1 us; the launch traced here: 48 us
  Pallas kernels  45.5 us (95%)
  between operations  1.29 us (3%)
  local copies, waits for them, and re-layouts  1.21 us (3%)
    pallas_call x1, Pallas kernels, on_device(): pl.pallas_call(functools.partial(kernel, slots), out_shape=(jax.ShapeDtyp...  45.5 us
    unnamed x2, local copies, waits for them, and re-layouts  1.21 us

profile of v2, /device:TPU:1, one launch (start us, length us, event | category | flops | bytes accessed | tf_op | source)
XLA Modules:
  0.0 48.0 jit_solution(9276575725327128584)
XLA Ops:
  1.3 45.5 %shard_map.77 = (f32[16,256]{1,0:T(8,128)S(1)}, f32[2,16,16]{2,1,0:T(8,128)S(1)}) custom-call(bf16[8,256]{1,0:T(8,128)(2,1)} %x_hbm.1, bf16[8,256]{1,0:T(8,128)(2,1)} %p_hbm.1, bf16[48,128,128]{2,1,0:T(8,128)(2,1)} %tiles_hbm.1, s32[1,48]{1,0:T(1,128)} %bitcast.2, s32[1,48]{1,0:T(1,128)} %bitcast.3, s32[1]{0:T(128)S(6)} %copy.10.count_s), custom_call_target="tpu_custom_call" | custom-call | tf_op jit(solution)/shard_map/pallas_call | solution.py:378
  46.8 0.6 %copy.11 = f32[16,256]{1,0:T(8,128)} copy(f32[16,256]{1,0:T(8,128)S(1)} %get-tuple-element.4) | data formatting | bytes 32768
  47.4 0.6 %copy.12 = f32[2,16,16]{2,1,0:T(8,128)} copy(f32[2,16,16]{2,1,0:T(8,128)S(1)} %get-tuple-element.5) | data formatting | bytes 4096

commit v3 on v2

--- a/solution.py
+++ b/solution.py
@@ -120,7 +120,7 @@
     friends = (
         [peer(dzl=i) for i in (1, 2, 3)]
         + [peer(dy=i) for i in (1, 2, 3)]
-        + [peer(dx=i) for i in (1, 2, 3)]
+        + [peer(dx=i, dc=dc) for i in (1, 2, 3) for dc in (0, 1)]
         + [peer(dzh=1), peer(dzh=3), peer(dc=1)]
     )
     for to in friends:
@@ -157,15 +157,12 @@
     far_x = []
 
     def far_spread(slot):
-        for i in (2, 1, 3):
+        block = far.at[pl.ds(slot * 2, 2)]
+        for n in (2, 6, 1, 3, 5, 7, 4):
+            i, dc = n % 4, n // 4
+            place = pl.ds(dc * 32 + (4 - i) % 4 * 8 + slot * 2, 2)
             far_x.append(
-                start(
-                    far.at[pl.ds(slot * 2, 2)],
-                    far.at[pl.ds((4 - i) * 8 + slot * 2, 2)],
-                    s_far_x.at[slot * 3 + i - 1],
-                    r_far_x.at[slot * 3 + i - 1],
-                    peer(dx=i),
-                )
+                start(block, far.at[place], s_far_x.at[slot * 7 + n - 1], r_far_x.at[slot * 7 + n - 1], peer(dx=i, dc=dc))
             )
 
     far_up = start(far.at[pl.ds(0, 2)], far.at[pl.ds(6, 2)], s_far.at[0], r_far.at[0], peer(dzh=1))
@@ -253,10 +250,10 @@
         out_ref[first : first + blocks] = (both[:, 0:TL] + both[:, TL : 2 * TL]).reshape(blocks, VB, TL)
 
     multiply(near, near_index, brow_s, NN)
+    far_two.wait_recv()
+    far_spread(2)
     scatter(kron_col, 32, 32, across_rows)
     core_rs = start(across_rows.at[pl.ds(32, 32)], core_in, s_row.at[0], r_row.at[0], peer(dc=1))
-    far_two.wait_recv()
-    far_spread(2)
     scatter(kron_col, 0, 32, across_rows)
     core_rs.wait_recv()
     x_rs = []
@@ -281,13 +278,16 @@
         both = lax.dot_general(both, vecs, NT, preferred_element_type=F32)
         return both[0:VB] + both[VB : 2 * VB]
 
-    for d in far_x[:9]:
+    wide = jnp.concatenate([near[b] for b in range(32)], axis=1)
+    tall = jnp.concatenate([eight(near[b]) for b in range(32)], axis=1)
+    fold_small(corr, 0, lax.dot_general(wide, tall, NT, preferred_element_type=F32))
+    corr_core = start(corr.at[0], corr_in.at[0], s_corr.at[0], r_corr.at[0], peer(dc=1))
+    for d in far_x[:21]:
         d.wait_recv()
     half = share([b for b in range(32) if b % 8 // 2 != 2])
-    for d in far_x[9:]:
+    for d in far_x[21:]:
         d.wait_recv()
     half = half + share([b for b in range(32) if b % 8 // 2 == 2])
-    far_core = start(far.at[pl.ds(0, 32)], far.at[pl.ds(32, 32)], s_far.at[6], r_far.at[6], peer(dc=1))
     fold_small(gram, 0, half)
     small_z = []
     for n in range(1, 16):
@@ -295,7 +295,9 @@
         to = (x * 8 + ((zz // 4) % 4) * 2 + core, y * 4 + zz % 4)
         small_z.append(start(gram.at[0], z_small.at[n - 1], s_small.at[n - 1], r_small.at[n - 1], to))
 
-    far_core.wait_recv()
+    corr_core.wait_recv()
+    corr[1] = corr[0] + corr_in[0]
+    corr_x = [start(corr.at[1], corr_in.at[i], s_corr.at[i], r_corr.at[i], peer(dx=i)) for i in (1, 2, 3)]
     multiply(far, far_index, bcol_s, NT)
     scatter(kron_row, 8, 24, down_rows)
     y_rs = []
@@ -306,10 +308,6 @@
             )
         )
     scatter(kron_row, 0, 8, down_rows)
-    wide = jnp.concatenate([near[b] for b in range(32)], axis=1)
-    tall = jnp.concatenate([eight(near[b]) for b in range(32)], axis=1)
-    fold_small(corr, 0, lax.dot_general(wide, tall, NT, preferred_element_type=F32))
-    corr_core = start(corr.at[0], corr_in.at[0], s_corr.at[0], r_corr.at[0], peer(dc=1))
     for d in x_rs:
         d.wait_recv()
     zh_rs = []
@@ -320,9 +318,10 @@
             zh_rs.append(
                 start(across_rows.at[mine], zh_in.at[pl.ds((i - 1) * 2, 2)], s_row.at[3 + i], r_row.at[3 + i], peer(dzh=i))
             )
-    corr_core.wait_recv()
-    corr[1] = corr[0] + corr_in[0]
-    corr_x = [start(corr.at[1], corr_in.at[i], s_corr.at[i], r_corr.at[i], peer(dx=i)) for i in (1, 2, 3)]
+    for d in corr_x:
+        d.wait_recv()
+    corr[2] = corr[1] + (corr_in[1] + corr_in[2] + corr_in[3])
+    corr_zh = [start(corr.at[2], corr_in.at[3 + i], s_corr.at[3 + i], r_corr.at[3 + i], peer(dzh=i)) for i in (1, 2, 3)]
 
     for d in y_rs:
         d.wait_recv()
@@ -335,11 +334,6 @@
                 start(down_rows.at[mine], zl_in.at[pl.ds((i - 1) * 2, 2)], s_col.at[3 + i], r_col.at[3 + i], peer(dzl=i))
             )
 
-    for d in corr_x:
-        d.wait_recv()
-    corr[2] = corr[1] + (corr_in[1] + corr_in[2] + corr_in[3])
-    corr_zh = [start(corr.at[2], corr_in.at[3 + i], s_corr.at[3 + i], r_corr.at[3 + i], peer(dzh=i)) for i in (1, 2, 3)]
-
     for d in small_z:
         d.wait_recv()
     gram[1] = gram[0] + jnp.sum(z_small[...], axis=0)
@@ -359,7 +353,7 @@
     small_ref[1] = unfold_small((corr[2] + (corr_in[4] + corr_in[5] + corr_in[6])) * scale)[0]
 
     for d in (
-        [far_up, far_dn, far_two, far_core, core_rs, corr_core]
+        [far_up, far_dn, far_two, core_rs, corr_core]
         + near_zl + near_y + far_x + x_rs + zh_rs + y_rs + zl_rs + corr_x + corr_zh + small_z
     ):
         d.wait_send()
@@ -413,10 +407,10 @@
             dma((4,)),
             dma((12,)),
             dma((12,)),
-            dma((7,)),
-            dma((7,)),
-            dma((12,)),
-            dma((12,)),
+            dma((3,)),
+            dma((3,)),
+            dma((28,)),
+            dma((28,)),
             dma((7,)),
             dma((7,)),
             dma((7,)),

time: 48.1 us -> 44.5 us (0.925)
  Pallas kernels: 45.5 us -> 41.9 us
    pallas_call x1, Pallas kernels: 45.5 us -> 41.9 us  [on_device(): pl.pallas_call(functools.partial(kernel, slots), out_shape=(jax.ShapeDtyp...]
where the time goes in v3:
time: 44.5 us; the launch traced here: 44.4 us
  Pallas kernels  41.9 us (94%)
  between operations  1.29 us (3%)
  local copies, waits for them, and re-layouts  1.21 us (3%)
    pallas_call x1, Pallas kernels, on_device(): pl.pallas_call(functools.partial(kernel, slots), out_shape=(jax.ShapeDtyp...  41.9 us
    unnamed x2, local copies, waits for them, and re-layouts  1.21 us

profile of v3, /device:TPU:1, one launch (start us, length us, event | category | flops | bytes accessed | tf_op | source)
XLA Modules:
  0.0 44.4 jit_solution(7287959928122935954)
XLA Ops:
  1.3 41.9 %shard_map.77 = (f32[16,256]{1,0:T(8,128)S(1)}, f32[2,16,16]{2,1,0:T(8,128)S(1)}) custom-call(bf16[8,256]{1,0:T(8,128)(2,1)} %x_hbm.1, bf16[8,256]{1,0:T(8,128)(2,1)} %p_hbm.1, bf16[48,128,128]{2,1,0:T(8,128)(2,1)} %tiles_hbm.1, s32[1,48]{1,0:T(1,128)} %bitcast.2, s32[1,48]{1,0:T(1,128)} %bitcast.3, s32[1]{0:T(128)S(6)} %copy.10.count_s), custom_call_target="tpu_custom_call" | custom-call | tf_op jit(solution)/shard_map/pallas_call | solution.py:372
  43.2 0.6 %copy.11 = f32[16,256]{1,0:T(8,128)} copy(f32[16,256]{1,0:T(8,128)S(1)} %get-tuple-element.4) | data formatting | bytes 32768
  43.8 0.6 %copy.12 = f32[2,16,16]{2,1,0:T(8,128)} copy(f32[2,16,16]{2,1,0:T(8,128)S(1)} %get-tuple-element.5) | data formatting | bytes 4096

commit v4 on v3

--- a/solution.py
+++ b/solution.py
@@ -81,8 +81,6 @@
     load_sem,
     s_near,
     r_near,
-    s_near_y,
-    r_near_y,
     s_far,
     r_far,
     s_far_x,
@@ -116,6 +114,12 @@
         desc.start()
         return desc
 
+    def received(region, sem):
+        copy(region, region, sem, sem, peer(dc=1)).wait_recv()
+
+    def left(region, sem):
+        copy(region, region, sem, sem, peer(dc=1)).wait_send()
+
     barrier = pltpu.get_barrier_semaphore()
     friends = (
         [peer(dzl=i) for i in (1, 2, 3)]
@@ -154,16 +158,13 @@
         far[b] = own
 
     pl.semaphore_wait(barrier, len(friends))
-    far_x = []
-
     def far_spread(slot):
         block = far.at[pl.ds(slot * 2, 2)]
         for n in (2, 6, 1, 3, 5, 7, 4):
             i, dc = n % 4, n // 4
             place = pl.ds(dc * 32 + (4 - i) % 4 * 8 + slot * 2, 2)
-            far_x.append(
-                start(block, far.at[place], s_far_x.at[slot * 7 + n - 1], r_far_x.at[slot * 7 + n - 1], peer(dx=i, dc=dc))
-            )
+            late = int(slot == 2)
+            start(block, far.at[place], s_far_x.at[late], r_far_x.at[late], peer(dx=i, dc=dc))
 
     far_up = start(far.at[pl.ds(0, 2)], far.at[pl.ds(6, 2)], s_far.at[0], r_far.at[0], peer(dzh=1))
     far_dn = start(far.at[pl.ds(0, 2)], far.at[pl.ds(2, 2)], s_far.at[1], r_far.at[1], peer(dzh=3))
@@ -172,19 +173,11 @@
         near_zl.append(
             start(near.at[pl.ds(0, 2)], near.at[pl.ds((4 - i) * 2, 2)], s_near.at[i], r_near.at[i], peer(dzl=i))
         )
-    near_y = []
 
     def near_spread(slot):
         for i in (2, 1, 3):
-            near_y.append(
-                start(
-                    near.at[pl.ds(slot * 2, 2)],
-                    near.at[pl.ds((4 - i) * 8 + slot * 2, 2)],
-                    s_near_y.at[slot * 3 + i - 1],
-                    r_near_y.at[slot * 3 + i - 1],
-                    peer(dy=i),
-                )
-            )
+            place = pl.ds((4 - i) * 8 + slot * 2, 2)
+            start(near.at[pl.ds(slot * 2, 2)], near.at[place], s_near.at[0], r_near.at[0], peer(dy=i))
 
     near_spread(0)
     far_spread(0)
@@ -232,8 +225,7 @@
     far_spread(1)
     build(kron_row, near_index(brow_v[...]), 32)
     fetches[6].wait()
-    for d in near_y:
-        d.wait_recv()
+    received(near.at[pl.ds(8, 24)], r_near.at[0])
 
     def multiply(vec_ref, index_of, index_s, dims):
         for k in range(slots):
@@ -256,19 +248,11 @@
     core_rs = start(across_rows.at[pl.ds(32, 32)], core_in, s_row.at[0], r_row.at[0], peer(dc=1))
     scatter(kron_col, 0, 32, across_rows)
     core_rs.wait_recv()
-    x_rs = []
     for i in (2, 1, 3, 0):
-        across_rows[i * 8 : i * 8 + 8] += core_in[i * 8 : i * 8 + 8]
+        mine = pl.ds(i * 8, 8)
+        across_rows[mine] += core_in[mine]
         if i:
-            x_rs.append(
-                start(
-                    across_rows.at[pl.ds(i * 8, 8)],
-                    x_in.at[pl.ds((i - 1) * 8, 8)],
-                    s_row.at[i],
-                    r_row.at[i],
-                    peer(dx=i),
-                )
-            )
+            start(across_rows.at[mine], x_in.at[pl.ds((i - 1) * 8, 8)], s_row.at[1], r_row.at[1], peer(dx=i))
 
     def share(blocks):
         high = [across_rows[b].astype(BF16) for b in blocks]
@@ -282,87 +266,76 @@
     tall = jnp.concatenate([eight(near[b]) for b in range(32)], axis=1)
     fold_small(corr, 0, lax.dot_general(wide, tall, NT, preferred_element_type=F32))
     corr_core = start(corr.at[0], corr_in.at[0], s_corr.at[0], r_corr.at[0], peer(dc=1))
-    for d in far_x[:21]:
-        d.wait_recv()
+    received(far.at[pl.ds(0, 42)], r_far_x.at[0])
     half = share([b for b in range(32) if b % 8 // 2 != 2])
-    for d in far_x[21:]:
-        d.wait_recv()
+    received(far.at[pl.ds(0, 14)], r_far_x.at[1])
     half = half + share([b for b in range(32) if b % 8 // 2 == 2])
     fold_small(gram, 0, half)
-    small_z = []
-    for n in range(1, 16):
+    for n in (8, 7, 9, 6, 10, 5, 11, 4, 12, 3, 13, 2, 14, 1, 15):
         zz = zh * 4 + zl + n
         to = (x * 8 + ((zz // 4) % 4) * 2 + core, y * 4 + zz % 4)
-        small_z.append(start(gram.at[0], z_small.at[n - 1], s_small.at[n - 1], r_small.at[n - 1], to))
+        start(gram.at[0], z_small.at[n - 1], s_small.at[0], r_small.at[0], to)
 
     corr_core.wait_recv()
     corr[1] = corr[0] + corr_in[0]
-    corr_x = [start(corr.at[1], corr_in.at[i], s_corr.at[i], r_corr.at[i], peer(dx=i)) for i in (1, 2, 3)]
+    for i in (1, 2, 3):
+        start(corr.at[1], corr_in.at[i], s_corr.at[1], r_corr.at[1], peer(dx=i))
     multiply(far, far_index, bcol_s, NT)
     scatter(kron_row, 8, 24, down_rows)
-    y_rs = []
     for i in (2, 1, 3):
-        y_rs.append(
-            start(
-                down_rows.at[pl.ds(i * 8, 8)], y_in.at[pl.ds((i - 1) * 8, 8)], s_col.at[i], r_col.at[i], peer(dy=i)
-            )
-        )
+        start(down_rows.at[pl.ds(i * 8, 8)], y_in.at[pl.ds((i - 1) * 8, 8)], s_col.at[0], r_col.at[0], peer(dy=i))
     scatter(kron_row, 0, 8, down_rows)
-    for d in x_rs:
-        d.wait_recv()
-    zh_rs = []
+    received(x_in, r_row.at[1])
     for i in (2, 1, 3, 0):
         mine = pl.ds(i * 2, 2)
         across_rows[mine] += x_in[i * 2 : i * 2 + 2] + x_in[8 + i * 2 : 10 + i * 2] + x_in[16 + i * 2 : 18 + i * 2]
         if i:
-            zh_rs.append(
-                start(across_rows.at[mine], zh_in.at[pl.ds((i - 1) * 2, 2)], s_row.at[3 + i], r_row.at[3 + i], peer(dzh=i))
-            )
-    for d in corr_x:
-        d.wait_recv()
+            start(across_rows.at[mine], zh_in.at[pl.ds((i - 1) * 2, 2)], s_row.at[2], r_row.at[2], peer(dzh=i))
+    received(corr_in.at[pl.ds(1, 3)], r_corr.at[1])
     corr[2] = corr[1] + (corr_in[1] + corr_in[2] + corr_in[3])
-    corr_zh = [start(corr.at[2], corr_in.at[3 + i], s_corr.at[3 + i], r_corr.at[3 + i], peer(dzh=i)) for i in (1, 2, 3)]
-
-    for d in y_rs:
-        d.wait_recv()
-    zl_rs = []
+    for i in (1, 2, 3):
+        start(corr.at[2], corr_in.at[3 + i], s_corr.at[2], r_corr.at[2], peer(dzh=i))
+
+    received(y_in, r_col.at[0])
     for i in (3, 2, 1, 0):
         mine = pl.ds(i * 2, 2)
         down_rows[mine] += y_in[i * 2 : i * 2 + 2] + y_in[8 + i * 2 : 10 + i * 2] + y_in[16 + i * 2 : 18 + i * 2]
         if i:
-            zl_rs.append(
-                start(down_rows.at[mine], zl_in.at[pl.ds((i - 1) * 2, 2)], s_col.at[3 + i], r_col.at[3 + i], peer(dzl=i))
-            )
-
-    for d in small_z:
-        d.wait_recv()
+            start(down_rows.at[mine], zl_in.at[pl.ds((i - 1) * 2, 2)], s_col.at[1], r_col.at[1], peer(dzl=i))
+
+    received(z_small, r_small.at[0])
     gram[1] = gram[0] + jnp.sum(z_small[...], axis=0)
-    small_xy = []
     for n in (20, 21, 4, 5, 16, 17, 12, 13, 18, 19, 22, 23, 28, 29, 2, 3, 6, 7, 8, 9, 24, 25, 10, 11, 14, 15, 26, 27, 30, 31, 1):
         to = peer(dx=n // 8, dy=(n // 2) % 4, dc=n % 2)
-        small_xy.append(start(gram.at[1], xy_small.at[n - 1], s_small.at[14 + n], r_small.at[14 + n], to))
+        start(gram.at[1], xy_small.at[n - 1], s_small.at[1], r_small.at[1], to)
 
     scale = 1.0 / (1024 * TL)
-    for d in zl_rs + zh_rs + corr_zh:
-        d.wait_recv()
+    received(zl_in, r_col.at[1])
+    received(zh_in, r_row.at[2])
     for b in range(2):
         images_ref[:, b * TL : (b + 1) * TL] = (
             (down_rows[b] + across_rows[b])
             + ((zl_in[b] + zl_in[2 + b] + zl_in[4 + b]) + (zh_in[b] + zh_in[2 + b] + zh_in[4 + b]))
         )
+    received(corr_in.at[pl.ds(4, 3)], r_corr.at[2])
     small_ref[1] = unfold_small((corr[2] + (corr_in[4] + corr_in[5] + corr_in[6])) * scale)[0]
 
-    for d in (
-        [far_up, far_dn, far_two, core_rs, corr_core]
-        + near_zl + near_y + far_x + x_rs + zh_rs + y_rs + zl_rs + corr_x + corr_zh + small_z
-    ):
+    for d in [far_up, far_dn, far_two, core_rs, corr_core] + near_zl:
         d.wait_send()
-    for d in small_xy:
-        d.wait_recv()
+    left(near.at[pl.ds(0, 24)], s_near.at[0])
+    left(far.at[pl.ds(0, 42)], s_far_x.at[0])
+    left(far.at[pl.ds(0, 14)], s_far_x.at[1])
+    left(x_in, s_row.at[1])
+    left(zh_in, s_row.at[2])
+    left(y_in, s_col.at[0])
+    left(zl_in, s_col.at[1])
+    left(corr_in.at[pl.ds(1, 3)], s_corr.at[1])
+    left(corr_in.at[pl.ds(4, 3)], s_corr.at[2])
+    left(z_small, s_small.at[0])
+    received(xy_small, r_small.at[1])
     straight, turned = unfold_small((gram[1] + jnp.sum(xy_small[...], axis=0)) * scale)
     small_ref[0] = straight + turned
-    for d in small_xy:
-        d.wait_send()
+    left(xy_small, s_small.at[1])
 
 
 def on_device(x_block, p_block, tile_values, tile_brow, tile_bcol, tile_count):
@@ -405,20 +378,18 @@
             dma((7,)),
             dma((4,)),
             dma((4,)),
-            dma((12,)),
-            dma((12,)),
-            dma((3,)),
-            dma((3,)),
-            dma((28,)),
-            dma((28,)),
-            dma((7,)),
-            dma((7,)),
-            dma((7,)),
-            dma((7,)),
-            dma((46,)),
-            dma((46,)),
-            dma((7,)),
-            dma((7,)),
+            dma((3,)),
+            dma((3,)),
+            dma((2,)),
+            dma((2,)),
+            dma((3,)),
+            dma((3,)),
+            dma((2,)),
+            dma((2,)),
+            dma((2,)),
+            dma((2,)),
+            dma((3,)),
+            dma((3,)),
         ],
         compiler_params=pltpu.CompilerParams(
             collective_id=0, has_side_effects=True, vmem_limit_bytes=32 * 2**20

time: 44.5 us -> 42.7 us (0.960)
  Pallas kernels: 41.9 us -> 40 us
    pallas_call x1, Pallas kernels: 41.9 us -> 40 us  [on_device(): pl.pallas_call(functools.partial(kernel, slots), out_shape=(jax.ShapeDtyp...]
where the time goes in v4:
time: 42.7 us; the launch traced here: 42.5 us
  Pallas kernels  40 us (94%)
  between operations  1.29 us (3%)
  local copies, waits for them, and re-layouts  1.21 us (3%)
    pallas_call x1, Pallas kernels, on_device(): pl.pallas_call(functools.partial(kernel, slots), out_shape=(jax.ShapeDtyp...  40 us
    unnamed x2, local copies, waits for them, and re-layouts  1.21 us

profile of v4, /device:TPU:1, one launch (start us, length us, event | category | flops | bytes accessed | tf_op | source)
XLA Modules:
  0.0 42.5 jit_solution(9111438239889214203)
XLA Ops:
  1.3 40.0 %shard_map.77 = (f32[16,256]{1,0:T(8,128)S(1)}, f32[2,16,16]{2,1,0:T(8,128)S(1)}) custom-call(bf16[8,256]{1,0:T(8,128)(2,1)} %x_hbm.1, bf16[8,256]{1,0:T(8,128)(2,1)} %p_hbm.1, bf16[48,128,128]{2,1,0:T(8,128)(2,1)} %tiles_hbm.1, s32[1,48]{1,0:T(1,128)} %bitcast.2, s32[1,48]{1,0:T(1,128)} %bitcast.3, s32[1]{0:T(128)S(6)} %copy.10.count_s), custom_call_target="tpu_custom_call" | custom-call | tf_op jit(solution)/shard_map/pallas_call | solution.py:345
  41.3 0.6 %copy.11 = f32[16,256]{1,0:T(8,128)} copy(f32[16,256]{1,0:T(8,128)S(1)} %get-tuple-element.4) | data formatting | bytes 32768
  41.9 0.6 %copy.12 = f32[2,16,16]{2,1,0:T(8,128)} copy(f32[2,16,16]{2,1,0:T(8,128)S(1)} %get-tuple-element.5) | data formatting | bytes 4096

commit v5 on v4

--- a/solution.py
+++ b/solution.py
@@ -122,10 +122,11 @@
 
     barrier = pltpu.get_barrier_semaphore()
     friends = (
-        [peer(dzl=i) for i in (1, 2, 3)]
-        + [peer(dy=i) for i in (1, 2, 3)]
-        + [peer(dx=i, dc=dc) for i in (1, 2, 3) for dc in (0, 1)]
-        + [peer(dzh=1), peer(dzh=3), peer(dc=1)]
+        [peer(dzh=1), peer(dzh=3)]
+        + [peer(dzl=i) for i in (3, 1, 2)]
+        + [peer(dy=i) for i in (2, 1, 3)]
+        + [peer(dx=i, dc=dc) for i in (2, 1, 3) for dc in (0, 1)]
+        + [peer(dc=1)]
     )
     for to in friends:
         pl.semaphore_signal(barrier, inc=1, device_id=to, device_id_type=MESH)
@@ -163,8 +164,7 @@
         for n in (2, 6, 1, 3, 5, 7, 4):
             i, dc = n % 4, n // 4
             place = pl.ds(dc * 32 + (4 - i) % 4 * 8 + slot * 2, 2)
-            late = int(slot == 2)
-            start(block, far.at[place], s_far_x.at[late], r_far_x.at[late], peer(dx=i, dc=dc))
+            start(block, far.at[place], s_far_x.at[0], r_far_x.at[0], peer(dx=i, dc=dc))
 
     far_up = start(far.at[pl.ds(0, 2)], far.at[pl.ds(6, 2)], s_far.at[0], r_far.at[0], peer(dzh=1))
     far_dn = start(far.at[pl.ds(0, 2)], far.at[pl.ds(2, 2)], s_far.at[1], r_far.at[1], peer(dzh=3))
@@ -215,13 +215,19 @@
     for fetch in fetches[2:6]:
         fetch.wait()
     build(kron_col, far_index(bcol_v[...]), 64)
-    for d, slot in zip(near_zl[::-1], (3, 2, 1)):
-        d.wait_recv()
-        near_spread(slot)
+    for j in range(3):
+        i = jnp.where(zl == 0, 3 - j, 1 + j)
+        received(near.at[pl.ds(0, 2)], r_near.at[i])
+        near_spread(4 - i)
     far_up.wait_recv()
-    far_two = start(far.at[pl.ds(6, 2)], far.at[pl.ds(4, 2)], s_far.at[2], r_far.at[2], peer(dzh=1))
+    far_dn.wait_recv()
+    for i in (2, 1, 3, 0):
+        spot = (4 - i) % 4 * 8 + 4
+        start(far.at[pl.ds(6, 1)], far.at[pl.ds(spot, 1)], s_far_x.at[1], r_far_x.at[1], peer(dx=i, dzh=1))
+    for i in (2, 1, 3, 0):
+        spot = (4 - i) % 4 * 8 + 5
+        start(far.at[pl.ds(3, 1)], far.at[pl.ds(spot, 1)], s_far_x.at[1], r_far_x.at[1], peer(dx=i, dzh=3))
     far_spread(3)
-    far_dn.wait_recv()
     far_spread(1)
     build(kron_row, near_index(brow_v[...]), 32)
     fetches[6].wait()
@@ -242,17 +248,15 @@
         out_ref[first : first + blocks] = (both[:, 0:TL] + both[:, TL : 2 * TL]).reshape(blocks, VB, TL)
 
     multiply(near, near_index, brow_s, NN)
-    far_two.wait_recv()
-    far_spread(2)
     scatter(kron_col, 32, 32, across_rows)
     core_rs = start(across_rows.at[pl.ds(32, 32)], core_in, s_row.at[0], r_row.at[0], peer(dc=1))
     scatter(kron_col, 0, 32, across_rows)
     core_rs.wait_recv()
-    for i in (2, 1, 3, 0):
-        mine = pl.ds(i * 8, 8)
-        across_rows[mine] += core_in[mine]
-        if i:
-            start(across_rows.at[mine], x_in.at[pl.ds((i - 1) * 8, 8)], s_row.at[1], r_row.at[1], peer(dx=i))
+    across_rows[0:32] += core_in[...]
+    for first, size, group in ((4, 2, 3), (0, 4, 1), (6, 2, 1)):
+        for i in (2, 1, 3):
+            mine, there = pl.ds(i * 8 + first, size), pl.ds((i - 1) * 8 + first, size)
+            start(across_rows.at[mine], x_in.at[there], s_row.at[group], r_row.at[group], peer(dx=i))
 
     def share(blocks):
         high = [across_rows[b].astype(BF16) for b in blocks]
@@ -268,7 +272,10 @@
     corr_core = start(corr.at[0], corr_in.at[0], s_corr.at[0], r_corr.at[0], peer(dc=1))
     received(far.at[pl.ds(0, 42)], r_far_x.at[0])
     half = share([b for b in range(32) if b % 8 // 2 != 2])
-    received(far.at[pl.ds(0, 14)], r_far_x.at[1])
+    received(far.at[pl.ds(0, 8)], r_far_x.at[1])
+    for i in range(4):
+        block = far.at[pl.ds(i * 8 + 4, 2)]
+        start(block, far.at[pl.ds(32 + i * 8 + 4, 2)], s_far.at[2], r_far.at[2], peer(dc=1))
     half = half + share([b for b in range(32) if b % 8 // 2 == 2])
     fold_small(gram, 0, half)
     for n in (8, 7, 9, 6, 10, 5, 11, 4, 12, 3, 13, 2, 14, 1, 15):
@@ -280,13 +287,18 @@
     corr[1] = corr[0] + corr_in[0]
     for i in (1, 2, 3):
         start(corr.at[1], corr_in.at[i], s_corr.at[1], r_corr.at[1], peer(dx=i))
+    received(far.at[pl.ds(0, 8)], r_far.at[2])
     multiply(far, far_index, bcol_s, NT)
     scatter(kron_row, 8, 24, down_rows)
-    for i in (2, 1, 3):
-        start(down_rows.at[pl.ds(i * 8, 8)], y_in.at[pl.ds((i - 1) * 8, 8)], s_col.at[0], r_col.at[0], peer(dy=i))
+    for first, size, group in ((2, 6, 0), (0, 2, 2)):
+        for i in (2, 1, 3):
+            mine, there = pl.ds(i * 8 + first, size), pl.ds((i - 1) * 8 + first, size)
+            start(down_rows.at[mine], y_in.at[there], s_col.at[group], r_col.at[group], peer(dy=i))
     scatter(kron_row, 0, 8, down_rows)
-    received(x_in, r_row.at[1])
+    received(x_in.at[pl.ds(0, 6)], r_row.at[3])
     for i in (2, 1, 3, 0):
+        if i == 1:
+            received(x_in.at[pl.ds(0, 18)], r_row.at[1])
         mine = pl.ds(i * 2, 2)
         across_rows[mine] += x_in[i * 2 : i * 2 + 2] + x_in[8 + i * 2 : 10 + i * 2] + x_in[16 + i * 2 : 18 + i * 2]
         if i:
@@ -296,8 +308,10 @@
     for i in (1, 2, 3):
         start(corr.at[2], corr_in.at[3 + i], s_corr.at[2], r_corr.at[2], peer(dzh=i))
 
-    received(y_in, r_col.at[0])
+    received(y_in.at[pl.ds(0, 18)], r_col.at[0])
     for i in (3, 2, 1, 0):
+        if i == 0:
+            received(y_in.at[pl.ds(0, 6)], r_col.at[2])
         mine = pl.ds(i * 2, 2)
         down_rows[mine] += y_in[i * 2 : i * 2 + 2] + y_in[8 + i * 2 : 10 + i * 2] + y_in[16 + i * 2 : 18 + i * 2]
         if i:
@@ -320,14 +334,17 @@
     received(corr_in.at[pl.ds(4, 3)], r_corr.at[2])
     small_ref[1] = unfold_small((corr[2] + (corr_in[4] + corr_in[5] + corr_in[6])) * scale)[0]
 
-    for d in [far_up, far_dn, far_two, core_rs, corr_core] + near_zl:
+    for d in [far_up, far_dn, core_rs, corr_core] + near_zl:
         d.wait_send()
     left(near.at[pl.ds(0, 24)], s_near.at[0])
     left(far.at[pl.ds(0, 42)], s_far_x.at[0])
-    left(far.at[pl.ds(0, 14)], s_far_x.at[1])
-    left(x_in, s_row.at[1])
+    left(far.at[pl.ds(0, 8)], s_far_x.at[1])
+    left(far.at[pl.ds(0, 8)], s_far.at[2])
+    left(x_in.at[pl.ds(0, 18)], s_row.at[1])
+    left(x_in.at[pl.ds(0, 6)], s_row.at[3])
     left(zh_in, s_row.at[2])
-    left(y_in, s_col.at[0])
+    left(y_in.at[pl.ds(0, 18)], s_col.at[0])
+    left(y_in.at[pl.ds(0, 6)], s_col.at[2])
     left(zl_in, s_col.at[1])
     left(corr_in.at[pl.ds(1, 3)], s_corr.at[1])
     left(corr_in.at[pl.ds(4, 3)], s_corr.at[2])
@@ -382,10 +399,10 @@
             dma((3,)),
             dma((2,)),
             dma((2,)),
-            dma((3,)),
-            dma((3,)),
-            dma((2,)),
-            dma((2,)),
+            dma((4,)),
+            dma((4,)),
+            dma((3,)),
+            dma((3,)),
             dma((2,)),
             dma((2,)),
             dma((3,)),

time: 42.7 us -> 41.3 us (0.967)
  Pallas kernels: 40 us -> 38.7 us
    pallas_call x1, Pallas kernels: 40 us -> 38.7 us  [on_device(): pl.pallas_call(functools.partial(kernel, slots), out_shape=(jax.ShapeDtyp...]
where the time goes in v5:
time: 41.3 us; the launch traced here: 41.2 us
  Pallas kernels  38.7 us (94%)
  between operations  1.29 us (3%)
  local copies, waits for them, and re-layouts  1.21 us (3%)
    pallas_call x1, Pallas kernels, on_device(): pl.pallas_call(functools.partial(kernel, slots), out_shape=(jax.ShapeDtyp...  38.7 us
    unnamed x2, local copies, waits for them, and re-layouts  1.21 us

profile of v5, /device:TPU:1, one launch (start us, length us, event | category | flops | bytes accessed | tf_op | source)
XLA Modules:
  0.0 41.2 jit_solution(14901138902529859090)
XLA Ops:
  1.3 38.7 %shard_map.77 = (f32[16,256]{1,0:T(8,128)S(1)}, f32[2,16,16]{2,1,0:T(8,128)S(1)}) custom-call(bf16[8,256]{1,0:T(8,128)(2,1)} %x_hbm.1, bf16[8,256]{1,0:T(8,128)(2,1)} %p_hbm.1, bf16[48,128,128]{2,1,0:T(8,128)(2,1)} %tiles_hbm.1, s32[1,48]{1,0:T(1,128)} %bitcast.2, s32[1,48]{1,0:T(1,128)} %bitcast.3, s32[1]{0:T(128)S(6)} %copy.10.count_s), custom_call_target="tpu_custom_call" | custom-call | tf_op jit(solution)/shard_map/pallas_call | solution.py:362
  40.0 0.6 %copy.11 = f32[16,256]{1,0:T(8,128)} copy(f32[16,256]{1,0:T(8,128)S(1)} %get-tuple-element.4) | data formatting | bytes 32768
  40.6 0.6 %copy.12 = f32[2,16,16]{2,1,0:T(8,128)} copy(f32[2,16,16]{2,1,0:T(8,128)S(1)} %get-tuple-element.5) | data formatting | bytes 4096

commit v6 on v5

--- a/solution.py
+++ b/solution.py
@@ -251,6 +251,10 @@
     scatter(kron_col, 32, 32, across_rows)
     core_rs = start(across_rows.at[pl.ds(32, 32)], core_in, s_row.at[0], r_row.at[0], peer(dc=1))
     scatter(kron_col, 0, 32, across_rows)
+    wide = jnp.concatenate([near[b] for b in range(32)], axis=1)
+    tall = jnp.concatenate([eight(near[b]) for b in range(32)], axis=1)
+    fold_small(corr, 0, lax.dot_general(wide, tall, NT, preferred_element_type=F32))
+    corr_core = start(corr.at[0], corr_in.at[0], s_corr.at[0], r_corr.at[0], peer(dc=1))
     core_rs.wait_recv()
     across_rows[0:32] += core_in[...]
     for first, size, group in ((4, 2, 3), (0, 4, 1), (6, 2, 1)):
@@ -266,10 +270,6 @@
         both = lax.dot_general(both, vecs, NT, preferred_element_type=F32)
         return both[0:VB] + both[VB : 2 * VB]
 
-    wide = jnp.concatenate([near[b] for b in range(32)], axis=1)
-    tall = jnp.concatenate([eight(near[b]) for b in range(32)], axis=1)
-    fold_small(corr, 0, lax.dot_general(wide, tall, NT, preferred_element_type=F32))
-    corr_core = start(corr.at[0], corr_in.at[0], s_corr.at[0], r_corr.at[0], peer(dc=1))
     received(far.at[pl.ds(0, 42)], r_far_x.at[0])
     half = share([b for b in range(32) if b % 8 // 2 != 2])
     received(far.at[pl.ds(0, 8)], r_far_x.at[1])

time: 41.3 us -> 41.1 us (level)
  no operation moved by 1% of the time
where the time goes in v6:
time: 41.1 us; the launch traced here: 41 us
  Pallas kernels  38.5 us (94%)
  between operations  1.29 us (3%)
  local copies, waits for them, and re-layouts  1.21 us (3%)
    pallas_call x1, Pallas kernels, on_device(): pl.pallas_call(functools.partial(kernel, slots), out_shape=(jax.ShapeDtyp...  38.5 us
    unnamed x2, local copies, waits for them, and re-layouts  1.21 us

profile of v6, /device:TPU:1, one launch (start us, length us, event | category | flops | bytes accessed | tf_op | source)
XLA Modules:
  0.0 41.0 jit_solution(13488422224336452638)
XLA Ops:
  1.3 38.5 %shard_map.77 = (f32[16,256]{1,0:T(8,128)S(1)}, f32[2,16,16]{2,1,0:T(8,128)S(1)}) custom-call(bf16[8,256]{1,0:T(8,128)(2,1)} %x_hbm.1, bf16[8,256]{1,0:T(8,128)(2,1)} %p_hbm.1, bf16[48,128,128]{2,1,0:T(8,128)(2,1)} %tiles_hbm.1, s32[1,48]{1,0:T(1,128)} %bitcast.2, s32[1,48]{1,0:T(1,128)} %bitcast.3, s32[1]{0:T(128)S(6)} %copy.10.count_s), custom_call_target="tpu_custom_call" | custom-call | tf_op jit(solution)/shard_map/pallas_call | solution.py:362
  39.8 0.6 %copy.11 = f32[16,256]{1,0:T(8,128)} copy(f32[16,256]{1,0:T(8,128)S(1)} %get-tuple-element.4) | data formatting | bytes 32768
  40.4 0.6 %copy.12 = f32[2,16,16]{2,1,0:T(8,128)} copy(f32[2,16,16]{2,1,0:T(8,128)S(1)} %get-tuple-element.5) | data formatting | bytes 4096
